TPU v7x, 32 devices: a whole 2x2x4 slice. The times are simulated.
32 devices in a mesh: seq: 8 (over y, x, core), enc: 4 (over z).
Axes of the slice: x: 2, y: 2, z: 4, core: 2. Of those that a mesh axis runs over, the one named last changes fastest.
Arguments:
- queries: bfloat16 [1024, 8192], P('seq', 'enc'), may hold values from -63 to 63
- image_key_value: bfloat16 [2, 32, 1601, 1024], P(None, ('seq', 'enc')), may hold values from -16 to 16
- image_spans: int32 [8, 2], replicated, may hold values from 0 to 1024, as said below
- tile_counts: int32 [8], replicated, may hold values from 1 to 4
- cross_gate: float32 [1], replicated, may hold values from 0.2 to 2
- grad_out: bfloat16 [1024, 8192], P('seq', 'enc'), may hold values from -6 to 6
Outputs:
- attended: bfloat16 [1024, 8192], P('seq', 'enc')
- grad_queries: bfloat16 [1024, 8192], P('seq', 'enc')
- grad_image_kv: bfloat16 [2, 32, 1601, 1024], P(None, ('seq', 'enc'))
Inputs may be any that keep to these rules, and one draw needn't show every extreme that they name: `image_spans`: image m owns tiles 4 m to 4 m + 3. Its span starts in text shard m (positions (m) * 128 to (m) * 128 + 127), starts do not fall from one image to the next within a shard, and each span holds 1 to 128 positions.
All inputs are finite; a program needn't handle non-finite values.
Results may differ from a plain program's by a relative error of at most 0.0062.
Values may be sent and summed in bfloat16 or wider, within the bound.
No kernel may reach another device: no remote copies, remote signals or barrier semaphores. Data moves between devices by JAX's collectives and lax.ppermute only.
A program may use at most 128 MiB of HBM per device.

v0:
```python
import functools

import jax
import jax.numpy as jnp
from jax import lax
from jax.experimental import pallas as pl
from jax.experimental.pallas import tpu as pltpu
from jax.sharding import PartitionSpec as P

HEAD_SIZE = 128
TILES = 4
LOW = -1e30
HIGH = 1e30
SCALE = HEAD_SIZE ** (-0.5)
LOG2E = 1.4426950408889634
BLOCK = 512
PAIR_ROWS = 256
TOGETHER = 2


def rotated(x, axis, by):
    total = lax.axis_size(axis)
    return lax.ppermute(x, axis, [(i, (i + by) % total) for i in range(total)])


def shifted(x, axis, by):
    total = lax.axis_size(axis)
    return lax.ppermute(x, axis, [(i, i + by) for i in range(total) if 0 <= i + by < total])


def dot_nt(a, b):
    return lax.dot_general(a, b, (((1,), (1,)), ((), ())), preferred_element_type=jnp.float32)


def dot_tn(a, b):
    return lax.dot_general(a, b, (((0,), (0,)), ((), ())), preferred_element_type=jnp.float32)


def dot_nn(a, b):
    return lax.dot_general(a, b, (((1,), (0,)), ((), ())), preferred_element_type=jnp.float32)


def stacked(ref, groups):
    return jnp.concatenate(
        [ref[0, :, i * HEAD_SIZE : (i + 1) * HEAD_SIZE] for i in range(groups)], axis=0
    )


def cuts(tokens):
    return [(start, min(BLOCK, tokens - start)) for start in range(0, tokens, BLOCK)]


def params():
    return pltpu.CompilerParams(vmem_limit_bytes=48 * 1024 * 1024)


def join_kernel(x_ref, o_ref):
    o_ref[:, 0, :] = x_ref[0]
    o_ref[:, 1, :] = x_ref[1]


def join_pairs(halves):
    _, tokens, width = halves.shape
    return pl.pallas_call(
        join_kernel,
        grid=(pl.cdiv(tokens, PAIR_ROWS),),
        in_specs=[pl.BlockSpec((2, PAIR_ROWS, width), lambda i: (0, i, 0))],
        out_specs=pl.BlockSpec((PAIR_ROWS, 2, width), lambda i: (i, 0, 0)),
        out_shape=jax.ShapeDtypeStruct((tokens, 2, width), halves.dtype),
        compiler_params=pltpu.CompilerParams(vmem_limit_bytes=16 * 1024 * 1024),
        cost_estimate=pl.CostEstimate(
            flops=0, bytes_accessed=4 * tokens * width * 4, transcendentals=0
        ),
        name="join_pairs",
    )(halves)


def forward_kernel(groups, at_ref, q_ref, k_ref, v_ref, o_ref, wide_ref, lse_ref, s_ref):
    parts = cuts(k_ref.shape[1])
    q = stacked(q_ref, groups)
    top = None
    for start, size in parts:
        s = dot_nt(k_ref[0, start : start + size], q)
        s_ref[start : start + size] = s
        peak = jnp.max(s, axis=0, keepdims=True)
        top = peak if top is None else jnp.maximum(top, peak)
    top = top * (SCALE * LOG2E)
    total = None
    out = None
    for start, size in parts:
        p = jnp.exp2(s_ref[start : start + size] * (SCALE * LOG2E) - top)
        part_total = jnp.sum(p, axis=0, keepdims=True)
        part_out = dot_tn(v_ref[0, start : start + size], p.astype(jnp.bfloat16))
        total = part_total if total is None else total + part_total
        out = part_out if out is None else out + part_out
    out = out / total
    lse = top + jnp.log2(total)
    wide_ref[0] = out
    for i in range(groups):
        span = slice(i * HEAD_SIZE, (i + 1) * HEAD_SIZE)
        o_ref[:, span] = out[:, span].T.astype(jnp.bfloat16)
        lse_ref[0, i : i + 1] = lse[:, span]


def delta_kernel(groups, at_ref, g_ref, wide_ref, delta_ref):
    for i in range(groups):
        span = slice(i * HEAD_SIZE, (i + 1) * HEAD_SIZE)
        g_t = g_ref[0, :, span].astype(jnp.float32).T
        delta_ref[0, i : i + 1] = jnp.sum(g_t * wide_ref[0, :, span], axis=0, keepdims=True)


def backward_kernel(groups, at_ref, q_ref, g_ref, k_ref, v_ref, lse_ref, delta_ref, *rest):
    dq_ref, dkv_ref = rest[-2:]
    k = k_ref[0]
    v = v_ref[0]
    lse_columns = lse_ref[0].T
    delta_columns = delta_ref[0].T
    dk = dv = None
    for first in range(0, groups, TOGETHER):
        members = range(first, first + TOGETHER)

        def rows(ref):
            return jnp.concatenate([ref[0, :, i * HEAD_SIZE : (i + 1) * HEAD_SIZE] for i in members], axis=0)

        def column(values):
            return jnp.concatenate([values[:, i : i + 1] for i in members], axis=0)

        q = rows(q_ref)
        g = rows(g_ref)
        w = jnp.exp2(dot_nt(q, k) * (SCALE * LOG2E) - column(lse_columns))
        ds = (w * (dot_nt(g, v) - column(delta_columns))).astype(jnp.bfloat16)
        dq = dot_nn(ds, k) * SCALE
        part_k = dot_tn(q, ds)
        part_v = dot_tn(g, w.astype(jnp.bfloat16))
        dk = part_k if dk is None else dk + part_k
        dv = part_v if dv is None else dv + part_v
        for i in members:
            start = (i - first) * dq_ref.shape[0]
            dq_ref[:, i * HEAD_SIZE : (i + 1) * HEAD_SIZE] = dq[start : start + dq_ref.shape[0]]
    dkv_ref[0] = (dk * SCALE).T.astype(jnp.bfloat16)
    dkv_ref[1] = dv.T.astype(jnp.bfloat16)


def row_spec(rows, groups):
    return pl.BlockSpec((1, rows.shape[1], groups * HEAD_SIZE), lambda h, at: (at[1], 0, h))


def image_specs(image_kv, heads):
    tokens = image_kv.shape[1]
    return [
        pl.BlockSpec((1, tokens, HEAD_SIZE), lambda h, at: (0, 0, at[0] * heads + h)),
        pl.BlockSpec((1, tokens, HEAD_SIZE), lambda h, at: (1, 0, at[0] * heads + h)),
    ]


def stat_spec(groups, text):
    return pl.BlockSpec((1, groups, text), lambda h, *at: (h, 0, 0))


def forward_call(at, q, image_kv, groups, heads):
    text = q.shape[1]
    width = groups * HEAD_SIZE
    tokens = image_kv.shape[1]
    lanes = groups * text
    return pl.pallas_call(
        functools.partial(forward_kernel, groups),
        grid_spec=pltpu.PrefetchScalarGridSpec(
            num_scalar_prefetch=1,
            grid=(heads,),
            in_specs=[row_spec(q, groups)] + image_specs(image_kv, heads),
            out_specs=[
                pl.BlockSpec((text, width), lambda h, at: (0, h)),
                pl.BlockSpec((1, HEAD_SIZE, lanes), lambda h, at: (h, 0, 0)),
                stat_spec(groups, text),
            ],
            scratch_shapes=[pltpu.VMEM((tokens + (-tokens) % 8, lanes), jnp.float32)],
        ),
        out_shape=[
            jax.ShapeDtypeStruct((text, heads * width), jnp.bfloat16),
            jax.ShapeDtypeStruct((heads, HEAD_SIZE, lanes), jnp.float32),
            jax.ShapeDtypeStruct((heads, groups, text), jnp.float32),
        ],
        compiler_params=params(),
        cost_estimate=pl.CostEstimate(
            flops=heads * 8 * tokens * lanes * HEAD_SIZE,
            bytes_accessed=heads * tokens * HEAD_SIZE * 4,
            transcendentals=heads * tokens * lanes,
        ),
        name="forward_group",
    )(at, q, image_kv, image_kv)


def delta_call(at, g, wide, groups, heads):
    text = g.shape[1]
    lanes = groups * text
    return pl.pallas_call(
        functools.partial(delta_kernel, groups),
        grid_spec=pltpu.PrefetchScalarGridSpec(
            num_scalar_prefetch=1,
            grid=(heads,),
            in_specs=[row_spec(g, groups), pl.BlockSpec((1, HEAD_SIZE, lanes), lambda h, at: (h, 0, 0))],
            out_specs=stat_spec(groups, text),
        ),
        out_shape=jax.ShapeDtypeStruct((heads, groups, text), jnp.float32),
        compiler_params=params(),
        cost_estimate=pl.CostEstimate(
            flops=heads * 2 * lanes * HEAD_SIZE, bytes_accessed=heads * lanes * HEAD_SIZE * 6, transcendentals=0
        ),
        name="delta_group",
    )(at, g, wide)


def backward_call(at, q, g, image_kv, lse, delta, grads, groups, heads):
    text = q.shape[1]
    width = groups * HEAD_SIZE
    tokens = image_kv.shape[1]
    lanes = groups * text
    stat = stat_spec(groups, text)
    in_specs = [row_spec(q, groups), row_spec(g, groups)] + image_specs(image_kv, heads) + [stat, stat]
    operands = [at, q, g, image_kv, image_kv, lse, delta]
    aliases = {}
    if grads is not None:
        in_specs.append(pl.BlockSpec(memory_space=pl.ANY))
        aliases = {len(operands): 1}
        operands.append(grads)
    return pl.pallas_call(
        functools.partial(backward_kernel, groups),
        grid_spec=pltpu.PrefetchScalarGridSpec(
            num_scalar_prefetch=1,
            grid=(heads,),
            in_specs=in_specs,
            out_specs=[
                pl.BlockSpec((text, width), lambda h, at: (0, h)),
                pl.BlockSpec((2, tokens, HEAD_SIZE), lambda h, at: (0, 0, at[0] * heads + h)),
            ],
        ),
        out_shape=[
            jax.ShapeDtypeStruct((text, heads * width), jnp.float32),
            jax.ShapeDtypeStruct(image_kv.shape, jnp.bfloat16),
        ],
        input_output_aliases=aliases,
        compiler_params=params(),
        cost_estimate=pl.CostEstimate(
            flops=heads * 20 * tokens * lanes * HEAD_SIZE,
            bytes_accessed=heads * tokens * HEAD_SIZE * 8,
            transcendentals=heads * tokens * lanes,
        ),
        name="backward_group",
    )(*operands)


def mix_kernel(groups, o_ref, own_ref, old_ref, carried_ref, out_ref):
    own = own_ref[0].T
    old = old_ref[0].T
    for i in range(groups):
        span = slice(i * HEAD_SIZE, (i + 1) * HEAD_SIZE)
        mix = o_ref[:, span].astype(jnp.float32) * own[:, i : i + 1]
        mix = mix + carried_ref[:, span].astype(jnp.float32) * old[:, i : i + 1]
        out_ref[:, span] = mix.astype(jnp.bfloat16)


def mix_call(out, own, old, carried):
    heads, groups, text = own.shape
    width = groups * HEAD_SIZE
    rows = pl.BlockSpec((text, width), lambda h: (0, h))
    return pl.pallas_call(
        functools.partial(mix_kernel, groups),
        grid=(heads,),
        in_specs=[rows, stat_spec(groups, text), stat_spec(groups, text), rows],
        out_specs=rows,
        out_shape=jax.ShapeDtypeStruct((text, heads * width), jnp.bfloat16),
        compiler_params=params(),
        cost_estimate=pl.CostEstimate(
            flops=4 * text * heads * width, bytes_accessed=6 * text * heads * width, transcendentals=0
        ),
        name="mix_group",
    )(out, own, old, carried)


def merged(lse, delta):
    top = jnp.max(lse, axis=0)
    share = jnp.exp2(lse - top)
    total = jnp.sum(share, axis=0)
    return top + jnp.log2(total), jnp.sum(share * delta, axis=0) / total


def shards(queries, image_key_value, image_spans, tile_counts, cross_gate, grad_out):
    seq_index = lax.axis_index("seq")
    seq_total = lax.axis_size("seq")
    enc_index = lax.axis_index("enc")
    enc_total = lax.axis_size("enc")
    text, width = queries.shape
    heads = image_key_value.shape[3] // (enc_total * HEAD_SIZE)
    groups = width // (heads * HEAD_SIZE)
    row_images = enc_total // TILES
    gate = jnp.tanh(cross_gate[0])
    steps = range(enc_total)

    spans = lax.dynamic_slice_in_dim(image_spans, seq_index * row_images, row_images, 0)
    offsets = spans[:, 0] - seq_index * text
    slots = jnp.arange(text, dtype=jnp.int32)
    in_own = slots[None, :] >= offsets[:, None]
    positions = jnp.where(in_own, seq_index * text, (seq_index + 1) * text) + slots[None, :]
    seen = (positions >= spans[:, :1]) & (positions < spans[:, 1:])

    sources = [lax.rem(enc_index - step + enc_total, enc_total) for step in steps]
    places = [source // TILES for source in sources]
    ats = [jnp.stack([source, places[0]]).astype(jnp.int32) for source in sources]
    counts = lax.dynamic_slice_in_dim(tile_counts, seq_index * row_images, row_images, 0)

    def of_place(x):
        return x[0] if row_images == 1 else lax.dynamic_index_in_dim(x, places[0], 0, False)

    def of_group(x, step):
        return lax.dynamic_index_in_dim(x, sources[step], 0, False)

    def placed(message, carried):
        if row_images == 1:
            return message
        base = jnp.zeros((row_images,) + message.shape, message.dtype) if carried is None else carried
        return lax.dynamic_update_index_in_dim(base, message, places[0], 0)

    in_use = (enc_index - places[0] * TILES) < of_place(counts)
    my_seen = of_place(seen) & in_use
    wide_own = in_own[:, None, None, None, :]
    order = jnp.stack(sources)

    def window(own, later):
        return jnp.where(in_own[:, :, None], own[None], later[None])

    middle = width // 2
    q_left, grad_out = lax.optimization_barrier((shifted(queries[:, :middle], "seq", -1), grad_out))
    q_later = jnp.concatenate([q_left, shifted(queries[:, middle:], "seq", -1)], axis=1)
    q_moving = window(queries, q_later)
    grad_mixed = (gate * grad_out.astype(jnp.float32)).astype(jnp.bfloat16)
    q_first, g_later, image_kv = lax.optimization_barrier(
        (q_moving, shifted(grad_mixed, "seq", -1), image_key_value)
    )
    q_rings = [q_first]
    g_rings = [window(grad_mixed, g_later)]
    image_kv = image_kv[:, 0]
    outs, wides, lse_ring, delta_ring = [], [], [], []
    for step in steps:
        more = step + 1 < enc_total
        if more:
            q_next = rotated(q_moving if step == 0 else q_rings[step], "enc", 1)
            if step == 0:
                q_next, image_kv = lax.optimization_barrier((q_next, image_kv))
            q_rings.append(q_next)
        out, wide, lse = forward_call(ats[step], q_rings[step], image_kv, groups, heads)
        outs.append(out)
        wides.append(wide)
        if step > 0:
            g_next, lse = lax.optimization_barrier((g_next, lse))
            g_rings.append(g_next)
        lse_ring.append(lse)
        if more:
            g_next = rotated(g_rings[step], "enc", 1)
        delta_ring.append(delta_call(ats[step], g_rings[step], wides[step], groups, heads))

    lse_mine = jnp.take(jnp.where(my_seen, jnp.stack(lse_ring), LOW), order, axis=0)
    delta_mine = jnp.take(jnp.stack(delta_ring), order, axis=0)
    mine = jnp.stack([lse_mine, delta_mine])
    early = row_images == 1
    tiles = [mine] + [rotated(mine, "enc", step) for step in steps[1:]]
    tile_lse = jnp.stack([t[0] for t in tiles])
    tile_delta = jnp.stack([t[1] for t in tiles])
    if early:
        first_out, tile_lse = lax.optimization_barrier((outs[1], tile_lse))
        mix_carried = rotated(first_out, "enc", 1)
    image_lse, image_delta = [], []
    for a in range(row_images):
        lse_a = tile_lse
        if row_images > 1:
            lse_a = jnp.where((jnp.stack(places) == a)[:, None, None, None, None], lse_a, LOW)
        lse_a, delta_a = merged(lse_a, tile_delta)
        image_lse.append(lse_a)
        image_delta.append(delta_a)
    image_lse, image_delta = jnp.stack(image_lse), jnp.stack(image_delta)
    upper = merged(jnp.where(wide_own, image_lse, LOW), image_delta)
    lower = merged(jnp.where(wide_own, LOW, image_lse), image_delta)
    lower, upper = lax.optimization_barrier((jnp.stack(lower), jnp.stack(upper)))
    from_before = shifted(lower, "seq", 1)
    from_after = shifted(upper, "seq", -1)
    if early:
        from_before, from_after, mix_carried = lax.optimization_barrier((from_before, from_after, mix_carried))
    before_lse = jnp.where(seq_index > 0, from_before[0], LOW)
    after_lse = jnp.where(seq_index < seq_total - 1, from_after[0], LOW)
    own_total = merged(jnp.stack([upper[0], before_lse]), jnp.stack([upper[1], from_before[1]]))
    next_total = merged(jnp.stack([lower[0], after_lse]), jnp.stack([lower[1], from_after[1]]))
    full_lse = jnp.where(wide_own, own_total[0], next_total[0])
    full_delta = jnp.where(wide_own, own_total[1], next_total[1])
    mine_share = jnp.where(my_seen, jnp.exp2(lse_mine - of_place(image_lse)), 0.0)
    home_share = jnp.where(full_lse > LOW / 2, jnp.exp2(image_lse - full_lse), 0.0) * gate
    lse_used = jnp.where(my_seen, of_place(full_lse), HIGH)
    delta_used = of_place(full_delta)

    def mixed(step, carried):
        share = of_group(mine_share, step)
        if carried is None:
            return mix_call(outs[step], share, share, jnp.zeros((text, width), jnp.bfloat16))
        old = jnp.ones_like(share)
        if early and step == 2:
            old = jnp.exp2(of_group(tile_lse[1], step) - of_group(of_place(image_lse), step))
        if early and step == 0:
            home = of_group(home_share[0], 0)
            share, old = share * home, old * home
        return mix_call(outs[step], share, old, of_place(carried) if row_images > 1 else carried)

    def homing(sums):
        sums = sums.reshape(row_images, text, width).astype(jnp.float32)
        kept = jnp.sum(jnp.where(in_own[:, :, None], sums, 0.0), axis=0)
        passed = jnp.sum(jnp.where(in_own[:, :, None], 0.0, sums), axis=0).astype(jnp.bfloat16)
        return kept, shifted(passed, "seq", 1)

    def homed(kept, passed):
        return (kept + passed.astype(jnp.float32)).astype(jnp.bfloat16)

    def scaled_home(sums):
        if early:
            return sums
        shares = jnp.stack([of_group(home_share[a], 0) for a in range(row_images)])
        shares = shares.reshape(row_images, heads * groups, text).transpose(0, 2, 1)
        parts = sums.reshape(row_images, text, heads * groups, HEAD_SIZE).astype(jnp.float32)
        return (parts * shares[..., None]).reshape(row_images, text, width).astype(jnp.bfloat16)

    if not early:
        mix_carried = rotated(placed(mixed(1, None), None), "enc", 1)
    mix_carried = placed(mixed(2, mix_carried), mix_carried)
    mix_moving = rotated(mix_carried, "enc", 1)
    grads = None
    carried = None
    for step in list(steps[1:]) + [0]:
        q = q_rings[step]
        grad_q, grads = backward_call(
            ats[step], q, g_rings[step], image_kv, of_group(lse_used, step), of_group(delta_used, step),
            grads, groups, heads,
        )
        if step == 0:
            grad_q, mix_passed = lax.optimization_barrier((grad_q, mix_passed))
        if carried is not None:
            grad_q = grad_q + (carried if row_images == 1 else of_place(carried)).astype(jnp.float32)
        carried = placed(grad_q.astype(jnp.bfloat16), carried)
        if step > 0:
            carried = rotated(carried, "enc", 1)
        if 0 < step < enc_total - 1:
            following = (step + 2) % enc_total
            if following == 0:
                continue
            mix_moving, grads = lax.optimization_barrier((mix_moving, grads))
            mix_carried = placed(mixed(following, mix_moving), mix_moving)
            mix_moving = rotated(mix_carried, "enc", 1)
        elif step > 0:
            mix_moving, grads = lax.optimization_barrier((mix_moving, grads))
            mix_carried = placed(mixed(0, mix_moving), mix_moving)
            mix_kept, mix_passed = homing(scaled_home(mix_carried))
    grads = join_pairs(grads).transpose(1, 0, 2).reshape(image_key_value.shape)

    grad_kept, grad_passed = homing(carried)
    return (homed(mix_kept, mix_passed), homed(grad_kept, grad_passed), grads)


def solution(mesh):
    in_specs = (
        P("seq", "enc"),
        P(None, ("seq", "enc"), None, None),
        P(),
        P(),
        P(),
        P("seq", "enc"),
    )
    out_specs = (P("seq", "enc"), P("seq", "enc"), P(None, ("seq", "enc"), None, None))
    return jax.shard_map(shards, mesh=mesh, in_specs=in_specs, out_specs=out_specs, check_vma=False)
```

profile of v0, /device:TPU:1, one launch (start us, length us, event | category | flops | bytes accessed | tf_op | source)
XLA Modules:
  0.0 195.6 jit_solution(5235559302722226278)
XLA Ops:
  1.7 2.0 %collective-permute-start = (bf16[128,1024]{1,0:T(8,128)(2,1)S(1)}, bf16[128,1024]{1,0:T(8,128)(2,1)S(1)}, u32[]{:S(2)}, u32[]{:S(2)}) collective-permute-start(bf16[128,1024]{1,0:T(8,128)(2,1)S(1)} %get-tuple-element.114), channel_id=1, source_target_pairs={{4,0},{8,4},{12,8},{16,12},{20,16},{24,20},{28,24},{5,1},{9,5},{13... | collective-permute-start | bytes 786440 | tf_op jit(solution)/shard_map/ppermute | solution.py:28
  7.7 2.5 %collective-permute-done = bf16[128,1024]{1,0:T(8,128)(2,1)S(1)} collective-permute-done((bf16[128,1024]{1,0:T(8,128)(2,1)S(1)}, bf16[128,1024]{1,0:T(8,128)(2,1)S(1)}, u32[]{:S(2)}, u32[]{:S(2)}) %collective-permute-start) | collective-permute-done | bytes 262176 | tf_op jit(solution)/shard_map/ppermute | solution.py:28
  17.9 4.3 %collective-permute-done.2 = bf16[128,2048]{1,0:T(8,128)(2,1)S(1)} collective-permute-done((bf16[128,2048]{1,0:T(8,128)(2,1)S(1)}, bf16[128,2048]{1,0:T(8,128)(2,1)S(1)}, u32[]{:S(2)}, u32[]{:S(2)}) %collective-permute-start.2) | collective-permute-done | bytes 524320 | tf_op jit(solution)/shard_map/ppermute | solution.py:28
  25.0 7.7 %copy.14 = bf16[2,1,1601,1024]{3,2,0,1:T(8,128)(2,1)} copy(bf16[2,1,1601,1024]{3,0,2,1:T(2,128)(2,1)} %param.9) | data formatting | bytes 13115392 | tf_op jit(solution)/shard_map/optimization_barrier | solution.py:336
  34.0 7.0 %forward_group.5 = (bf16[128,2048]{1,0:T(8,128)(2,1)S(1)}, f32[2,128,1024]{2,1,0:T(8,128)S(1)}, f32[2,8,128]{2,1,0:T(8,128)S(1)}) custom-call(s32[2]{0:T(128)S(1)} %get-tuple-element.151.at_ref, bf16[1,128,2048]{2,1,0:T(8,128)(2,1)S(1)} %collective-permute-done.3.q_ref, bf16[2,1601,1024]{2,1,0:T(8,128)(2,1)} %bitcast.103, bf16[2,1601,1024]{2,1,0:T(8,128)(2,1)} %bitcast.104), custom_call_target="tpu_custom_call" | custom-call | flops 3357540352 | bytes 1639424 | tf_op jit(solution)/shard_map/forward_group/pallas_call | solution.py:165
  45.0 9.9 %collective-permute-done.6.q_ref = bf16[1,128,2048]{2,1,0:T(8,128)(2,1)S(1)} collective-permute-done((bf16[1,128,2048]{2,1,0:T(8,128)(2,1)S(1)}, bf16[1,128,2048]{2,1,0:T(8,128)(2,1)S(1)}, u32[]{:S(2)}, u32[]{:S(2)}) %collective-permute-start.6) | collective-permute-done | bytes 524320 | tf_op jit(solution)/shard_map/ppermute | solution.py:23
  54.9 7.0 %forward_group.6 = (bf16[128,2048]{1,0:T(8,128)(2,1)S(1)}, f32[2,128,1024]{2,1,0:T(8,128)S(1)}, f32[2,8,128]{2,1,0:T(8,128)S(1)}) custom-call(s32[2]{0:T(128)S(1)} %pad_add_fusion.2.at_ref, bf16[1,128,2048]{2,1,0:T(8,128)(2,1)S(1)} %collective-permute-done.6.q_ref, bf16[2,1601,1024]{2,1,0:T(8,128)(2,1)} %bitcast.105, bf16[2,1601,1024]{2,1,0:T(8,128)(2,1)} %bitcast.106), custom_call_target="tpu_custom_call" | custom-call | flops 3357540352 | bytes 1639424 | tf_op jit(solution)/shard_map/forward_group/pallas_call | solution.py:165
  61.9 4.3 %collective-permute-done.5.g_ref = bf16[1,128,2048]{2,1,0:T(8,128)(2,1)S(1)} collective-permute-done((bf16[1,128,2048]{2,1,0:T(8,128)(2,1)S(1)}, bf16[1,128,2048]{2,1,0:T(8,128)(2,1)S(1)}, u32[]{:S(2)}, u32[]{:S(2)}) %collective-permute-start.5) | collective-permute-done | bytes 524320 | tf_op jit(solution)/shard_map/ppermute | solution.py:23
  66.2 7.0 %forward_group.4 = (bf16[128,2048]{1,0:T(8,128)(2,1)S(1)}, f32[2,128,1024]{2,1,0:T(8,128)S(1)}, f32[2,8,128]{2,1,0:T(8,128)S(1)}) custom-call(s32[2]{0:T(128)S(1)} %get-tuple-element.150.at_ref, bf16[1,128,2048]{2,1,0:T(8,128)(2,1)S(1)} %fusion.6.q_ref, bf16[2,1601,1024]{2,1,0:T(8,128)(2,1)} %bitcast.107, bf16[2,1601,1024]{2,1,0:T(8,128)(2,1)} %bitcast.108), custom_call_target="tpu_custom_call" | custom-call | flops 3357540352 | bytes 1639424 | tf_op jit(solution)/shard_map/forward_group/pallas_call | solution.py:165
  77.4 7.0 %forward_group.7 = (bf16[128,2048]{1,0:T(8,128)(2,1)S(1)}, f32[2,128,1024]{2,1,0:T(8,128)S(1)}, f32[2,8,128]{2,1,0:T(8,128)S(1)}) custom-call(s32[2]{0:T(128)S(1)} %pad_add_fusion.3.at_ref, bf16[1,128,2048]{2,1,0:T(8,128)(2,1)S(1)} %collective-permute-done.8.q_ref, bf16[2,1601,1024]{2,1,0:T(8,128)(2,1)} %bitcast.109, bf16[2,1601,1024]{2,1,0:T(8,128)(2,1)} %bitcast.110), custom_call_target="tpu_custom_call" | custom-call | flops 3357540352 | bytes 1639424 | tf_op jit(solution)/shard_map/forward_group/pallas_call | solution.py:165
  91.4 4.0 %collective-permute-done.10 = f32[2,4,2,8,128]{4,3,2,1,0:T(8,128)S(1)} collective-permute-done((f32[2,4,2,8,128]{4,3,2,1,0:T(8,128)S(1)}, f32[2,4,2,8,128]{4,3,2,1,0:T(8,128)S(1)}, u32[]{:S(2)}, u32[]{:S(2)}) %collective-permute-start.10) | collective-permute-done | bytes 65568 | tf_op jit(solution)/shard_map/ppermute | solution.py:23
  95.8 2.3 %collective-permute-start.13 = (f32[2,4,2,8,128]{4,3,2,1,0:T(8,128)S(1)}, f32[2,4,2,8,128]{4,3,2,1,0:T(8,128)S(1)}, u32[]{:S(2)}, u32[]{:S(2)}) collective-permute-start(f32[2,4,2,8,128]{4,3,2,1,0:T(8,128)S(1)} %pad_maximum_fusion.3), channel_id=1, source_target_pairs={{4,0},{8,4},{12,8},{16,12},{20,16},{24,20},{28,24},{5,1},{9,5},{13... | collective-permute-start | bytes 196616 | tf_op jit(solution)/shard_map/ppermute | solution.py:28
  98.1 8.1 %collective-permute-start.12 = (f32[2,4,2,8,128]{4,3,2,1,0:T(8,128)S(1)}, f32[2,4,2,8,128]{4,3,2,1,0:T(8,128)S(1)}, u32[]{:S(2)}, u32[]{:S(2)}) collective-permute-start(f32[2,4,2,8,128]{4,3,2,1,0:T(8,128)S(1)} %pad_maximum_fusion.2), channel_id=1, source_target_pairs={{0,4},{4,8},{8,12},{12,16},{16,20},{20,24},{24,28},{1,5},{5,9},{9,... | collective-permute-start | bytes 196616 | tf_op jit(solution)/shard_map/ppermute | solution.py:28
  107.5 3.3 %collective-permute-done.14.carried_ref = bf16[128,2048]{1,0:T(8,128)(2,1)S(1)} collective-permute-done((bf16[128,2048]{1,0:T(8,128)(2,1)}, bf16[128,2048]{1,0:T(8,128)(2,1)S(1)}, u32[]{:S(2)}, u32[]{:S(2)}) %collective-permute-start.14) | collective-permute-done | bytes 524320 | tf_op jit(solution)/shard_map/ppermute | solution.py:23
  114.4 11.2 %backward_group.4 = (f32[128,2048]{1,0:T(8,128)S(1)}, bf16[2,1601,1024]{2,1,0:T(8,128)(2,1)}) custom-call(s32[2]{0:T(128)S(1)} %get-tuple-element.151.at_ref, bf16[1,128,2048]{2,1,0:T(8,128)(2,1)S(1)} %copy-done.11, bf16[1,128,2048]{2,1,0:T(8,128)(2,1)S(1)} %copy-done.5, bf16[2,1601,1024]{2,1,0:T(8,128)(2,1)} %bitcast.111, bf16[2,1601,1024]{2,1,0:T(8,128)(2,1)} %bitcast.112, ...), custom_call_target="tpu_custom_call" | custom-call | flops 8393850880 | bytes 3278848 | tf_op jit(solution)/shard_map/backward_group/pallas_call | solution.py:226
  127.9 11.1 %backward_group.5 = (f32[128,2048]{1,0:T(8,128)S(1)}, bf16[2,1601,1024]{2,1,0:T(8,128)(2,1)}) custom-call(s32[2]{0:T(128)S(1)} %pad_add_fusion.2.at_ref, bf16[1,128,2048]{2,1,0:T(8,128)(2,1)S(1)} %copy-done.7, bf16[1,128,2048]{2,1,0:T(8,128)(2,1)S(1)} %collective-permute-done.5.g_ref, ...), custom_call_target="tpu_custom_call", output_to_operand_aliasing={{1}: (7, {})} | custom-call | flops 8393850880 | bytes 3278848 | tf_op jit(solution)/shard_map/backward_group/pallas_call | solution.py:226
  139.7 2.5 %collective-permute-start.19 = (bf16[128,2048]{1,0:T(8,128)(2,1)S(1)}, bf16[128,2048]{1,0:T(8,128)(2,1)S(1)}, u32[]{:S(2)}, u32[]{:S(2)}) collective-permute-start(bf16[128,2048]{1,0:T(8,128)(2,1)S(1)} %add_convert_fusion.2), channel_id=1, source_target_pairs={{0,1},{1,2},{2,3},{3,0},{4,5},{5,6},{6,7},{7,4},{8,9},{9,10},{10,1... | collective-permute-start | bytes 1572872 | tf_op jit(solution)/shard_map/ppermute | solution.py:23
  142.3 11.1 %backward_group.6 = (f32[128,2048]{1,0:T(8,128)S(1)}, bf16[2,1601,1024]{2,1,0:T(8,128)(2,1)}) custom-call(s32[2]{0:T(128)S(1)} %pad_add_fusion.3.at_ref, bf16[1,128,2048]{2,1,0:T(8,128)(2,1)S(1)} %copy-done.9, bf16[1,128,2048]{2,1,0:T(8,128)(2,1)S(1)} %copy-done.3, bf16[2,1601,1024]{2,1,0:T(8,128)(2,1)} %bitcast.115, ...), custom_call_target="tpu_custom_call", output_to_operand_aliasing={{1}: (7, {})} | custom-call | flops 8393850880 | bytes 3278848 | tf_op jit(solution)/shard_map/backward_group/pallas_call | solution.py:226
  154.8 9.9 %collective-permute-start.17 = (bf16[128,2048]{1,0:T(8,128)(2,1)S(1)}, bf16[128,2048]{1,0:T(8,128)(2,1)S(1)}, u32[]{:S(2)}, u32[]{:S(2)}) collective-permute-start(bf16[128,2048]{1,0:T(8,128)(2,1)S(1)} %fusion.2), channel_id=1, source_target_pairs={{0,4},{4,8},{8,12},{12,16},{16,20},{20,24},{24,28},{1,5},{5,9},{9,... | collective-permute-start | bytes 1572872 | tf_op jit(solution)/shard_map/ppermute | solution.py:28
  165.2 11.2 %backward_group.7 = (f32[128,2048]{1,0:T(8,128)S(1)}, bf16[2,1601,1024]{2,1,0:T(8,128)(2,1)}) custom-call(s32[2]{0:T(128)S(1)} %get-tuple-element.150.at_ref, bf16[1,128,2048]{2,1,0:T(8,128)(2,1)S(1)} %fusion.6.q_ref, bf16[1,128,2048]{2,1,0:T(8,128)(2,1)S(1)} %select_bitcast_fusion.g_ref, ...), custom_call_target="tpu_custom_call", output_to_operand_aliasing={{1}: (7, {})} | custom-call | flops 8393850880 | bytes 3278848 | tf_op jit(solution)/shard_map/backward_group/pallas_call | solution.py:226
  176.4 4.5 %collective-permute-done.20 = bf16[128,2048]{1,0:T(8,128)(2,1)S(1)} collective-permute-done((bf16[128,2048]{1,0:T(8,128)(2,1)S(1)}, bf16[128,2048]{1,0:T(8,128)(2,1)S(1)}, u32[]{:S(2)}, u32[]{:S(2)}) %collective-permute-start.20) | collective-permute-done | bytes 524320 | tf_op jit(solution)/shard_map/ppermute | solution.py:23
  181.0 4.3 %collective-permute-start.21 = (bf16[128,2048]{1,0:T(8,128)(2,1)S(1)}, bf16[128,2048]{1,0:T(8,128)(2,1)S(1)}, u32[]{:S(2)}, u32[]{:S(2)}) collective-permute-start(bf16[128,2048]{1,0:T(8,128)(2,1)S(1)} %fusion.5), channel_id=1, source_target_pairs={{0,4},{4,8},{8,12},{12,16},{16,20},{20,24},{24,28},{1,5},{5,9},{9,... | collective-permute-start | bytes 1572872 | tf_op jit(solution)/shard_map/ppermute | solution.py:28
  185.4 2.9 %copy-done.1 = bf16[2,1601,1024]{2,1,0:T(8,128)(2,1)S(1)} copy-done((bf16[2,1601,1024]{2,1,0:T(8,128)(2,1)S(1)}, bf16[2,1601,1024]{2,1,0:T(8,128)(2,1)}, u32[]{:S(2)}) %copy-start.1) | copy-done | bytes 6557720
  188.2 5.8 %join_pairs.1 = bf16[1601,2,1024]{2,1,0:T(2,128)(2,1)} custom-call(bf16[2,1601,1024]{2,1,0:T(8,128)(2,1)S(1)} %copy-done.1), custom_call_target="tpu_custom_call" | custom-call | bytes 26230784 | tf_op jit(solution)/shard_map/join_pairs/pallas_call | solution.py:64
  (112 shorter events, 41.5 us)
Async XLA Ops:
  1.7 8.6 %collective-permute-start = (bf16[128,1024]{1,0:T(8,128)(2,1)S(1)}, bf16[128,1024]{1,0:T(8,128)(2,1)S(1)}, u32[]{:S(2)}, u32[]{:S(2)}) collective-permute-start(bf16[128,1024]{1,0:T(8,128)(2,1)S(1)} %get-tuple-element.114), channel_id=1, source_target_pairs={{4,0},{8,4},{12,8},{16,12},{20,16},{24,20},{28,24},{5,1},{9,5},{13... | collective-permute-start | bytes 786440 | tf_op jit(solution)/shard_map/ppermute | solution.py:28
  3.7 11.6 %collective-permute-start.1 = (bf16[128,1024]{1,0:T(8,128)(2,1)S(1)}, bf16[128,1024]{1,0:T(8,128)(2,1)S(1)}, u32[]{:S(2)}, u32[]{:S(2)}) collective-permute-start(bf16[128,1024]{1,0:T(8,128)(2,1)S(1)} %get-tuple-element.115), channel_id=1, source_target_pairs={{4,0},{8,4},{12,8},{16,12},{20,16},{24,20},{28,24},{5,1},{9,5},{13... | collective-permute-start | bytes 786440 | tf_op jit(solution)/shard_map/ppermute | solution.py:28
  11.4 10.8 %collective-permute-start.2 = (bf16[128,2048]{1,0:T(8,128)(2,1)S(1)}, bf16[128,2048]{1,0:T(8,128)(2,1)S(1)}, u32[]{:S(2)}, u32[]{:S(2)}) collective-permute-start(bf16[128,2048]{1,0:T(8,128)(2,1)S(1)} %multiply_convert_fusion), channel_id=1, source_target_pairs={{4,0},{8,4},{12,8},{16,12},{20,16},{24,20},{28,24},{5,1},{9,5},{13... | collective-permute-start | bytes 1572872 | tf_op jit(solution)/shard_map/ppermute | solution.py:28
  16.5 16.1 %collective-permute-start.3 = (bf16[1,128,2048]{2,1,0:T(8,128)(2,1)S(1)}, bf16[1,128,2048]{2,1,0:T(8,128)(2,1)S(1)}, u32[]{:S(2)}, u32[]{:S(2)}) collective-permute-start(bf16[1,128,2048]{2,1,0:T(8,128)(2,1)S(1)} %fusion.6.q_ref), channel_id=1, source_target_pairs={{0,1},{1,2},{2,3},{3,0},{4,5},{5,6},{6,7},{7,4},{8,9},{9,10},{10,1... | collective-permute-start | bytes 1572872 | tf_op jit(solution)/shard_map/ppermute | solution.py:23
  23.5 20.2 %collective-permute-start.4 = (bf16[1,128,2048]{2,1,0:T(8,128)(2,1)S(1)}, bf16[1,128,2048]{2,1,0:T(8,128)(2,1)S(1)}, u32[]{:S(2)}, u32[]{:S(2)}) collective-permute-start(bf16[1,128,2048]{2,1,0:T(8,128)(2,1)S(1)} %select_bitcast_fusion.g_ref), channel_id=1, source_target_pairs={{0,1},{1,2},{2,3},{3,0},{4,5},{5,6},{6,7},{7,4},{8,9},{9,10},{10,1... | collective-permute-start | bytes 1572872 | tf_op jit(solution)/shard_map/ppermute | solution.py:23
  32.7 22.2 %collective-permute-start.6 = (bf16[1,128,2048]{2,1,0:T(8,128)(2,1)S(1)}, bf16[1,128,2048]{2,1,0:T(8,128)(2,1)S(1)}, u32[]{:S(2)}, u32[]{:S(2)}) collective-permute-start(bf16[1,128,2048]{2,1,0:T(8,128)(2,1)S(1)} %collective-permute-done.3.q_ref), channel_id=1, source_target_pairs={{0,1},{1,2},{2,3},{3,0},{4,5},{5,6},{6,7},{7,4},{8,9},{9,10},{10,1... | collective-permute-start | bytes 1572872 | tf_op jit(solution)/shard_map/ppermute | solution.py:23
  43.7 30.4 %copy-start.4 = (bf16[1,128,2048]{2,1,0:T(8,128)(2,1)}, bf16[1,128,2048]{2,1,0:T(8,128)(2,1)S(1)}, u32[]{:S(2)}) copy-start(bf16[1,128,2048]{2,1,0:T(8,128)(2,1)S(1)} %collective-permute-done.4.g_ref) | copy-start | bytes 1572868
  43.7 22.5 %collective-permute-start.5 = (bf16[1,128,2048]{2,1,0:T(8,128)(2,1)S(1)}, bf16[1,128,2048]{2,1,0:T(8,128)(2,1)S(1)}, u32[]{:S(2)}, u32[]{:S(2)}) collective-permute-start(bf16[1,128,2048]{2,1,0:T(8,128)(2,1)S(1)} %collective-permute-done.4.g_ref), channel_id=1, source_target_pairs={{0,1},{1,2},{2,3},{3,0},{4,5},{5,6},{6,7},{7,4},{8,9},{9,10},{10,1... | collective-permute-start | bytes 1572872 | tf_op jit(solution)/shard_map/ppermute | solution.py:23
  54.9 22.5 %collective-permute-start.8 = (bf16[1,128,2048]{2,1,0:T(8,128)(2,1)S(1)}, bf16[1,128,2048]{2,1,0:T(8,128)(2,1)S(1)}, u32[]{:S(2)}, u32[]{:S(2)}) collective-permute-start(bf16[1,128,2048]{2,1,0:T(8,128)(2,1)S(1)} %collective-permute-done.6.q_ref), channel_id=1, source_target_pairs={{0,1},{1,2},{2,3},{3,0},{4,5},{5,6},{6,7},{7,4},{8,9},{9,10},{10,1... | collective-permute-start | bytes 1572872 | tf_op jit(solution)/shard_map/ppermute | solution.py:23
  66.2 19.3 %collective-permute-start.7 = (bf16[1,128,2048]{2,1,0:T(8,128)(2,1)S(1)}, bf16[1,128,2048]{2,1,0:T(8,128)(2,1)S(1)}, u32[]{:S(2)}, u32[]{:S(2)}) collective-permute-start(bf16[1,128,2048]{2,1,0:T(8,128)(2,1)S(1)} %collective-permute-done.5.g_ref), channel_id=1, source_target_pairs={{0,1},{1,2},{2,3},{3,0},{4,5},{5,6},{6,7},{7,4},{8,9},{9,10},{10,1... | collective-permute-start | bytes 1572872 | tf_op jit(solution)/shard_map/ppermute | solution.py:23
  87.7 3.8 %collective-permute-start.11 = (f32[2,4,2,8,128]{4,3,2,1,0:T(8,128)S(1)}, f32[2,4,2,8,128]{4,3,2,1,0:T(8,128)S(1)}, u32[]{:S(2)}, u32[]{:S(2)}) collective-permute-start(f32[2,4,2,8,128]{4,3,2,1,0:T(8,128)S(1)} %pad_maximum_fusion.1), channel_id=1, source_target_pairs={{0,3},{1,0},{2,1},{3,2},{4,7},{5,4},{6,5},{7,6},{8,11},{9,8},{10,9... | collective-permute-start | bytes 196616 | tf_op jit(solution)/shard_map/ppermute | solution.py:23
  89.5 6.0 %collective-permute-start.10 = (f32[2,4,2,8,128]{4,3,2,1,0:T(8,128)S(1)}, f32[2,4,2,8,128]{4,3,2,1,0:T(8,128)S(1)}, u32[]{:S(2)}, u32[]{:S(2)}) collective-permute-start(f32[2,4,2,8,128]{4,3,2,1,0:T(8,128)S(1)} %pad_maximum_fusion.1), channel_id=1, source_target_pairs={{0,2},{1,3},{2,0},{3,1},{4,6},{5,7},{6,4},{7,5},{8,10},{9,11},{10,... | collective-permute-start | bytes 196616 | tf_op jit(solution)/shard_map/ppermute | solution.py:23
  89.5 6.0 %collective-permute-start.9 = (f32[2,4,2,8,128]{4,3,2,1,0:T(8,128)S(1)}, f32[2,4,2,8,128]{4,3,2,1,0:T(8,128)S(1)}, u32[]{:S(2)}, u32[]{:S(2)}) collective-permute-start(f32[2,4,2,8,128]{4,3,2,1,0:T(8,128)S(1)} %pad_maximum_fusion.1), channel_id=1, source_target_pairs={{0,1},{1,2},{2,3},{3,0},{4,5},{5,6},{6,7},{7,4},{8,9},{9,10},{10,1... | collective-permute-start | bytes 196616 | tf_op jit(solution)/shard_map/ppermute | solution.py:23
  95.6 15.2 %collective-permute-start.14 = (bf16[128,2048]{1,0:T(8,128)(2,1)}, bf16[128,2048]{1,0:T(8,128)(2,1)S(1)}, u32[]{:S(2)}, u32[]{:S(2)}) collective-permute-start(bf16[128,2048]{1,0:T(8,128)(2,1)} %copy-done.12), channel_id=1, source_target_pairs={{0,1},{1,2},{2,3},{3,0},{4,5},{5,6},{6,7},{7,4},{8,9},{9,10},{10,1... | collective-permute-start | bytes 1572872 | tf_op jit(solution)/shard_map/ppermute | solution.py:23
  95.8 10.7 %collective-permute-start.13 = (f32[2,4,2,8,128]{4,3,2,1,0:T(8,128)S(1)}, f32[2,4,2,8,128]{4,3,2,1,0:T(8,128)S(1)}, u32[]{:S(2)}, u32[]{:S(2)}) collective-permute-start(f32[2,4,2,8,128]{4,3,2,1,0:T(8,128)S(1)} %pad_maximum_fusion.3), channel_id=1, source_target_pairs={{4,0},{8,4},{12,8},{16,12},{20,16},{24,20},{28,24},{5,1},{9,5},{13... | collective-permute-start | bytes 196616 | tf_op jit(solution)/shard_map/ppermute | solution.py:28
  98.1 9.4 %collective-permute-start.12 = (f32[2,4,2,8,128]{4,3,2,1,0:T(8,128)S(1)}, f32[2,4,2,8,128]{4,3,2,1,0:T(8,128)S(1)}, u32[]{:S(2)}, u32[]{:S(2)}) collective-permute-start(f32[2,4,2,8,128]{4,3,2,1,0:T(8,128)S(1)} %pad_maximum_fusion.2), channel_id=1, source_target_pairs={{0,4},{4,8},{8,12},{12,16},{16,20},{20,24},{24,28},{1,5},{5,9},{9,... | collective-permute-start | bytes 196616 | tf_op jit(solution)/shard_map/ppermute | solution.py:28
  112.2 14.0 %collective-permute-start.15 = (bf16[128,2048]{1,0:T(8,128)(2,1)S(1)}, bf16[128,2048]{1,0:T(8,128)(2,1)S(1)}, u32[]{:S(2)}, u32[]{:S(2)}) collective-permute-start(bf16[128,2048]{1,0:T(8,128)(2,1)S(1)} %mix_group.3), channel_id=1, source_target_pairs={{0,1},{1,2},{2,3},{3,0},{4,5},{5,6},{6,7},{7,4},{8,9},{9,10},{10,1... | collective-permute-start | bytes 1572872 | tf_op jit(solution)/shard_map/ppermute | solution.py:23
  125.6 14.0 %collective-permute-start.18 = (bf16[128,2048]{1,0:T(8,128)(2,1)S(1)}, bf16[128,2048]{1,0:T(8,128)(2,1)S(1)}, u32[]{:S(2)}, u32[]{:S(2)}) collective-permute-start(bf16[128,2048]{1,0:T(8,128)(2,1)S(1)} %convert_element_type.59), channel_id=1, source_target_pairs={{0,1},{1,2},{2,3},{3,0},{4,5},{5,6},{6,7},{7,4},{8,9},{9,10},{10,1... | collective-permute-start | bytes 1572872 | tf_op jit(solution)/shard_map/ppermute | solution.py:23
  127.4 26.0 %collective-permute-start.16 = (bf16[128,2048]{1,0:T(8,128)(2,1)S(1)}, bf16[128,2048]{1,0:T(8,128)(2,1)S(1)}, u32[]{:S(2)}, u32[]{:S(2)}) collective-permute-start(bf16[128,2048]{1,0:T(8,128)(2,1)S(1)} %mix_group.4), channel_id=1, source_target_pairs={{0,1},{1,2},{2,3},{3,0},{4,5},{5,6},{6,7},{7,4},{8,9},{9,10},{10,1... | collective-permute-start | bytes 1572872 | tf_op jit(solution)/shard_map/ppermute | solution.py:23
  127.9 14.4 %copy-start.9 = (bf16[1,128,2048]{2,1,0:T(8,128)(2,1)S(1)}, bf16[1,128,2048]{2,1,0:T(8,128)(2,1)}, u32[]{:S(2)}) copy-start(bf16[1,128,2048]{2,1,0:T(8,128)(2,1)} %copy-done.8) | copy-start | bytes 1572868
  139.7 25.0 %collective-permute-start.19 = (bf16[128,2048]{1,0:T(8,128)(2,1)S(1)}, bf16[128,2048]{1,0:T(8,128)(2,1)S(1)}, u32[]{:S(2)}, u32[]{:S(2)}) collective-permute-start(bf16[128,2048]{1,0:T(8,128)(2,1)S(1)} %add_convert_fusion.2), channel_id=1, source_target_pairs={{0,1},{1,2},{2,3},{3,0},{4,5},{5,6},{6,7},{7,4},{8,9},{9,10},{10,1... | collective-permute-start | bytes 1572872 | tf_op jit(solution)/shard_map/ppermute | solution.py:23
  154.8 21.6 %collective-permute-start.17 = (bf16[128,2048]{1,0:T(8,128)(2,1)S(1)}, bf16[128,2048]{1,0:T(8,128)(2,1)S(1)}, u32[]{:S(2)}, u32[]{:S(2)}) collective-permute-start(bf16[128,2048]{1,0:T(8,128)(2,1)S(1)} %fusion.2), channel_id=1, source_target_pairs={{0,4},{4,8},{8,12},{12,16},{16,20},{20,24},{24,28},{1,5},{5,9},{9,... | collective-permute-start | bytes 1572872 | tf_op jit(solution)/shard_map/ppermute | solution.py:28
  164.8 16.0 %collective-permute-start.20 = (bf16[128,2048]{1,0:T(8,128)(2,1)S(1)}, bf16[128,2048]{1,0:T(8,128)(2,1)S(1)}, u32[]{:S(2)}, u32[]{:S(2)}) collective-permute-start(bf16[128,2048]{1,0:T(8,128)(2,1)S(1)} %add_convert_fusion.1), channel_id=1, source_target_pairs={{0,1},{1,2},{2,3},{3,0},{4,5},{5,6},{6,7},{7,4},{8,9},{9,10},{10,1... | collective-permute-start | bytes 1572872 | tf_op jit(solution)/shard_map/ppermute | solution.py:23
  181.0 13.0 %collective-permute-start.21 = (bf16[128,2048]{1,0:T(8,128)(2,1)S(1)}, bf16[128,2048]{1,0:T(8,128)(2,1)S(1)}, u32[]{:S(2)}, u32[]{:S(2)}) collective-permute-start(bf16[128,2048]{1,0:T(8,128)(2,1)S(1)} %fusion.5), channel_id=1, source_target_pairs={{0,4},{4,8},{8,12},{12,16},{16,20},{20,24},{24,28},{1,5},{5,9},{9,... | collective-permute-start | bytes 1572872 | tf_op jit(solution)/shard_map/ppermute | solution.py:28
  (11 other events, 61.9 us)
where the time goes:
time: 196 us
  Pallas kernels  85.5 us (44%)
  waiting for transfers between devices  41.2 us (21%)
  starting transfers between devices  40.2 us (21%)
  local copies, waits for them, and re-layouts  17.6 us (9%)
  other arithmetic  7.8 us (4%)
  between operations  3.18 us (2%)
    pallas_call x4, Pallas kernels, backward_call(): pl.pallas_call(functools.partial(backward_kernel, groups), grid_spec=pltp...  44.6 us
    ppermute x15, waiting for transfers between devices, rotated(): return lax.ppermute(x, axis, [(i, (i + by) % total) for i in range(total)])  33.1 us
    ppermute x7, starting transfers between devices, shifted(): lax.ppermute(x, axis, [(i, i + by) for i in range(total) if 0 <= i + by <...  30.4 us
    pallas_call x4, Pallas kernels, forward_call(): pl.pallas_call(functools.partial(forward_kernel, groups), grid_spec=pltpu...  27.8 us
    ppermute x15, starting transfers between devices, rotated(): return lax.ppermute(x, axis, [(i, (i + by) % total) for i in range(total)])  9.74 us
    ppermute x7, waiting for transfers between devices, shifted(): lax.ppermute(x, axis, [(i, i + by) for i in range(total) if 0 <= i + by <...  8.15 us
    optimization_barrier x1, local copies, waits for them, and re-layouts, shards(): lax.optimization_barrier((q_moving, shifted(grad_mixed, 'seq', -1), image...  7.72 us
    unnamed x26, local copies, waits for them, and re-layouts  5.82 us
  transfers between devices with their start and end apart: 22, of which 15 were waited for; matrix products, arithmetic and copies ran while one was open for 8% of the time, Pallas kernels for 43%

commit v1 on v0

--- a/solution.py
+++ b/solution.py
@@ -13,9 +13,8 @@
 HIGH = 1e30
 SCALE = HEAD_SIZE ** (-0.5)
 LOG2E = 1.4426950408889634
-BLOCK = 512
 PAIR_ROWS = 256
-TOGETHER = 2
+TOGETHER = 4
 
 
 def rotated(x, axis, by):
@@ -44,10 +43,6 @@
     return jnp.concatenate(
         [ref[0, :, i * HEAD_SIZE : (i + 1) * HEAD_SIZE] for i in range(groups)], axis=0
     )
-
-
-def cuts(tokens):
-    return [(start, min(BLOCK, tokens - start)) for start in range(0, tokens, BLOCK)]
 
 
 def params():
@@ -76,24 +71,12 @@
 
 
 def forward_kernel(groups, at_ref, q_ref, k_ref, v_ref, o_ref, wide_ref, lse_ref, s_ref):
-    parts = cuts(k_ref.shape[1])
-    q = stacked(q_ref, groups)
-    top = None
-    for start, size in parts:
-        s = dot_nt(k_ref[0, start : start + size], q)
-        s_ref[start : start + size] = s
-        peak = jnp.max(s, axis=0, keepdims=True)
-        top = peak if top is None else jnp.maximum(top, peak)
-    top = top * (SCALE * LOG2E)
-    total = None
-    out = None
-    for start, size in parts:
-        p = jnp.exp2(s_ref[start : start + size] * (SCALE * LOG2E) - top)
-        part_total = jnp.sum(p, axis=0, keepdims=True)
-        part_out = dot_tn(v_ref[0, start : start + size], p.astype(jnp.bfloat16))
-        total = part_total if total is None else total + part_total
-        out = part_out if out is None else out + part_out
-    out = out / total
+    s = dot_nt(k_ref[0], stacked(q_ref, groups))
+    s_ref[...] = s
+    top = jnp.max(s, axis=0, keepdims=True) * (SCALE * LOG2E)
+    p = jnp.exp2(s_ref[...] * (SCALE * LOG2E) - top)
+    total = jnp.sum(p, axis=0, keepdims=True)
+    out = dot_tn(v_ref[0], p.astype(jnp.bfloat16)) / total
     lse = top + jnp.log2(total)
     wide_ref[0] = out
     for i in range(groups):
@@ -173,7 +156,7 @@
                 pl.BlockSpec((1, HEAD_SIZE, lanes), lambda h, at: (h, 0, 0)),
                 stat_spec(groups, text),
             ],
-            scratch_shapes=[pltpu.VMEM((tokens + (-tokens) % 8, lanes), jnp.float32)],
+            scratch_shapes=[pltpu.VMEM((tokens, lanes), jnp.float32)],
         ),
         out_shape=[
             jax.ShapeDtypeStruct((text, heads * width), jnp.bfloat16),

time: 196 us -> 196 us (level)
  transfers between devices with their start and end apart: 22 -> 22, of which waited for: 15 -> 15; matrix products, arithmetic and copies ran while one was open for 8% -> 8% of each run, Pallas kernels for 43% -> 42%
where the time goes in v1:
time: 196 us
  Pallas kernels  84.3 us (43%)
  waiting for transfers between devices  42.4 us (22%)
  starting transfers between devices  40.2 us (21%)
  local copies, waits for them, and re-layouts  17.6 us (9%)
  other arithmetic  7.8 us (4%)
  between operations  3.18 us (2%)
    pallas_call x4, Pallas kernels, backward_call(): pl.pallas_call(functools.partial(backward_kernel, groups), grid_spec=pltp...  44.5 us
    ppermute x15, waiting for transfers between devices, rotated(): return lax.ppermute(x, axis, [(i, (i + by) % total) for i in range(total)])  34.2 us
    ppermute x7, starting transfers between devices, shifted(): lax.ppermute(x, axis, [(i, i + by) for i in range(total) if 0 <= i + by <...  30.6 us
    pallas_call x4, Pallas kernels, forward_call(): pl.pallas_call(functools.partial(forward_kernel, groups), grid_spec=pltpu...  26.8 us
    ppermute x15, starting transfers between devices, rotated(): return lax.ppermute(x, axis, [(i, (i + by) % total) for i in range(total)])  9.64 us
    ppermute x7, waiting for transfers between devices, shifted(): lax.ppermute(x, axis, [(i, i + by) for i in range(total) if 0 <= i + by <...  8.15 us
    optimization_barrier x1, local copies, waits for them, and re-layouts, shards(): lax.optimization_barrier((q_moving, shifted(grad_mixed, 'seq', -1), image...  7.72 us
    unnamed x26, local copies, waits for them, and re-layouts  5.82 us
  transfers between devices with their start and end apart: 22, of which 15 were waited for; matrix products, arithmetic and copies ran while one was open for 8% of the time, Pallas kernels for 42%

profile of v1, /device:TPU:1, one launch (start us, length us, event | category | flops | bytes accessed | tf_op | source)
XLA Modules:
  0.0 195.5 jit_solution(3350585009101707897)
XLA Ops:
  7.7 2.5 %collective-permute-done = bf16[128,1024]{1,0:T(8,128)(2,1)S(1)} collective-permute-done((bf16[128,1024]{1,0:T(8,128)(2,1)S(1)}, bf16[128,1024]{1,0:T(8,128)(2,1)S(1)}, u32[]{:S(2)}, u32[]{:S(2)}) %collective-permute-start) | collective-permute-done | bytes 262176 | tf_op jit(solution)/shard_map/ppermute | solution.py:27
  17.9 4.3 %collective-permute-done.2 = bf16[128,2048]{1,0:T(8,128)(2,1)S(1)} collective-permute-done((bf16[128,2048]{1,0:T(8,128)(2,1)S(1)}, bf16[128,2048]{1,0:T(8,128)(2,1)S(1)}, u32[]{:S(2)}, u32[]{:S(2)}) %collective-permute-start.2) | collective-permute-done | bytes 524320 | tf_op jit(solution)/shard_map/ppermute | solution.py:27
  25.0 7.7 %copy.14 = bf16[2,1,1601,1024]{3,2,0,1:T(8,128)(2,1)} copy(bf16[2,1,1601,1024]{3,0,2,1:T(2,128)(2,1)} %param.9) | data formatting | bytes 13115392 | tf_op jit(solution)/shard_map/optimization_barrier | solution.py:319
  34.0 6.7 %forward_group.5 = (bf16[128,2048]{1,0:T(8,128)(2,1)S(1)}, f32[2,128,1024]{2,1,0:T(8,128)S(1)}, f32[2,8,128]{2,1,0:T(8,128)S(1)}) custom-call(s32[2]{0:T(128)S(1)} %get-tuple-element.151.at_ref, bf16[1,128,2048]{2,1,0:T(8,128)(2,1)S(1)} %collective-permute-done.3.q_ref, bf16[2,1601,1024]{2,1,0:T(8,128)(2,1)} %bitcast.103, bf16[2,1601,1024]{2,1,0:T(8,128)(2,1)} %bitcast.104), custom_call_target="tpu_custom_call" | custom-call | flops 3357540352 | bytes 1639424 | tf_op jit(solution)/shard_map/forward_group/pallas_call | solution.py:148
  41.6 2.1 %collective-permute-done.4.g_ref = bf16[1,128,2048]{2,1,0:T(8,128)(2,1)S(1)} collective-permute-done((bf16[1,128,2048]{2,1,0:T(8,128)(2,1)S(1)}, bf16[1,128,2048]{2,1,0:T(8,128)(2,1)S(1)}, u32[]{:S(2)}, u32[]{:S(2)}) %collective-permute-start.4) | collective-permute-done | bytes 524320 | tf_op jit(solution)/shard_map/ppermute | solution.py:22
  45.0 9.9 %collective-permute-done.6.q_ref = bf16[1,128,2048]{2,1,0:T(8,128)(2,1)S(1)} collective-permute-done((bf16[1,128,2048]{2,1,0:T(8,128)(2,1)S(1)}, bf16[1,128,2048]{2,1,0:T(8,128)(2,1)S(1)}, u32[]{:S(2)}, u32[]{:S(2)}) %collective-permute-start.6) | collective-permute-done | bytes 524320 | tf_op jit(solution)/shard_map/ppermute | solution.py:22
  54.9 6.7 %forward_group.6 = (bf16[128,2048]{1,0:T(8,128)(2,1)S(1)}, f32[2,128,1024]{2,1,0:T(8,128)S(1)}, f32[2,8,128]{2,1,0:T(8,128)S(1)}) custom-call(s32[2]{0:T(128)S(1)} %pad_add_fusion.2.at_ref, bf16[1,128,2048]{2,1,0:T(8,128)(2,1)S(1)} %collective-permute-done.6.q_ref, bf16[2,1601,1024]{2,1,0:T(8,128)(2,1)} %bitcast.105, bf16[2,1601,1024]{2,1,0:T(8,128)(2,1)} %bitcast.106), custom_call_target="tpu_custom_call" | custom-call | flops 3357540352 | bytes 1639424 | tf_op jit(solution)/shard_map/forward_group/pallas_call | solution.py:148
  61.6 4.5 %collective-permute-done.5.g_ref = bf16[1,128,2048]{2,1,0:T(8,128)(2,1)S(1)} collective-permute-done((bf16[1,128,2048]{2,1,0:T(8,128)(2,1)S(1)}, bf16[1,128,2048]{2,1,0:T(8,128)(2,1)S(1)}, u32[]{:S(2)}, u32[]{:S(2)}) %collective-permute-start.5) | collective-permute-done | bytes 524320 | tf_op jit(solution)/shard_map/ppermute | solution.py:22
  66.2 6.7 %forward_group.4 = (bf16[128,2048]{1,0:T(8,128)(2,1)S(1)}, f32[2,128,1024]{2,1,0:T(8,128)S(1)}, f32[2,8,128]{2,1,0:T(8,128)S(1)}) custom-call(s32[2]{0:T(128)S(1)} %get-tuple-element.150.at_ref, bf16[1,128,2048]{2,1,0:T(8,128)(2,1)S(1)} %fusion.6.q_ref, bf16[2,1601,1024]{2,1,0:T(8,128)(2,1)} %bitcast.107, bf16[2,1601,1024]{2,1,0:T(8,128)(2,1)} %bitcast.108), custom_call_target="tpu_custom_call" | custom-call | flops 3357540352 | bytes 1639424 | tf_op jit(solution)/shard_map/forward_group/pallas_call | solution.py:148
  77.4 6.7 %forward_group.7 = (bf16[128,2048]{1,0:T(8,128)(2,1)S(1)}, f32[2,128,1024]{2,1,0:T(8,128)S(1)}, f32[2,8,128]{2,1,0:T(8,128)S(1)}) custom-call(s32[2]{0:T(128)S(1)} %pad_add_fusion.3.at_ref, bf16[1,128,2048]{2,1,0:T(8,128)(2,1)S(1)} %collective-permute-done.8.q_ref, bf16[2,1601,1024]{2,1,0:T(8,128)(2,1)} %bitcast.109, bf16[2,1601,1024]{2,1,0:T(8,128)(2,1)} %bitcast.110), custom_call_target="tpu_custom_call" | custom-call | flops 3357540352 | bytes 1639424 | tf_op jit(solution)/shard_map/forward_group/pallas_call | solution.py:148
  91.4 4.0 %collective-permute-done.10 = f32[2,4,2,8,128]{4,3,2,1,0:T(8,128)S(1)} collective-permute-done((f32[2,4,2,8,128]{4,3,2,1,0:T(8,128)S(1)}, f32[2,4,2,8,128]{4,3,2,1,0:T(8,128)S(1)}, u32[]{:S(2)}, u32[]{:S(2)}) %collective-permute-start.10) | collective-permute-done | bytes 65568 | tf_op jit(solution)/shard_map/ppermute | solution.py:22
  95.8 2.3 %collective-permute-start.13 = (f32[2,4,2,8,128]{4,3,2,1,0:T(8,128)S(1)}, f32[2,4,2,8,128]{4,3,2,1,0:T(8,128)S(1)}, u32[]{:S(2)}, u32[]{:S(2)}) collective-permute-start(f32[2,4,2,8,128]{4,3,2,1,0:T(8,128)S(1)} %pad_maximum_fusion.3), channel_id=1, source_target_pairs={{4,0},{8,4},{12,8},{16,12},{20,16},{24,20},{28,24},{5,1},{9,5},{13... | collective-permute-start | bytes 196616 | tf_op jit(solution)/shard_map/ppermute | solution.py:27
  98.1 8.1 %collective-permute-start.12 = (f32[2,4,2,8,128]{4,3,2,1,0:T(8,128)S(1)}, f32[2,4,2,8,128]{4,3,2,1,0:T(8,128)S(1)}, u32[]{:S(2)}, u32[]{:S(2)}) collective-permute-start(f32[2,4,2,8,128]{4,3,2,1,0:T(8,128)S(1)} %pad_maximum_fusion.2), channel_id=1, source_target_pairs={{0,4},{4,8},{8,12},{12,16},{16,20},{20,24},{24,28},{1,5},{5,9},{9,... | collective-permute-start | bytes 196616 | tf_op jit(solution)/shard_map/ppermute | solution.py:27
  107.5 3.3 %collective-permute-done.14.carried_ref = bf16[128,2048]{1,0:T(8,128)(2,1)S(1)} collective-permute-done((bf16[128,2048]{1,0:T(8,128)(2,1)}, bf16[128,2048]{1,0:T(8,128)(2,1)S(1)}, u32[]{:S(2)}, u32[]{:S(2)}) %collective-permute-start.14) | collective-permute-done | bytes 524320 | tf_op jit(solution)/shard_map/ppermute | solution.py:22
  114.4 11.1 %backward_group.4 = (f32[128,2048]{1,0:T(8,128)S(1)}, bf16[2,1601,1024]{2,1,0:T(8,128)(2,1)}) custom-call(s32[2]{0:T(128)S(1)} %get-tuple-element.151.at_ref, bf16[1,128,2048]{2,1,0:T(8,128)(2,1)S(1)} %copy-done.11, bf16[1,128,2048]{2,1,0:T(8,128)(2,1)S(1)} %copy-done.5, bf16[2,1601,1024]{2,1,0:T(8,128)(2,1)} %bitcast.111, bf16[2,1601,1024]{2,1,0:T(8,128)(2,1)} %bitcast.112, ...), custom_call_target="tpu_custom_call" | custom-call | flops 8393850880 | bytes 3278848 | tf_op jit(solution)/shard_map/backward_group/pallas_call | solution.py:209
  127.8 11.1 %backward_group.5 = (f32[128,2048]{1,0:T(8,128)S(1)}, bf16[2,1601,1024]{2,1,0:T(8,128)(2,1)}) custom-call(s32[2]{0:T(128)S(1)} %pad_add_fusion.2.at_ref, bf16[1,128,2048]{2,1,0:T(8,128)(2,1)S(1)} %copy-done.7, bf16[1,128,2048]{2,1,0:T(8,128)(2,1)S(1)} %collective-permute-done.5.g_ref, ...), custom_call_target="tpu_custom_call", output_to_operand_aliasing={{1}: (7, {})} | custom-call | flops 8393850880 | bytes 3278848 | tf_op jit(solution)/shard_map/backward_group/pallas_call | solution.py:209
  139.7 2.5 %collective-permute-start.19 = (bf16[128,2048]{1,0:T(8,128)(2,1)S(1)}, bf16[128,2048]{1,0:T(8,128)(2,1)S(1)}, u32[]{:S(2)}, u32[]{:S(2)}) collective-permute-start(bf16[128,2048]{1,0:T(8,128)(2,1)S(1)} %add_convert_fusion.2), channel_id=1, source_target_pairs={{0,1},{1,2},{2,3},{3,0},{4,5},{5,6},{6,7},{7,4},{8,9},{9,10},{10,1... | collective-permute-start | bytes 1572872 | tf_op jit(solution)/shard_map/ppermute | solution.py:22
  142.2 11.1 %backward_group.6 = (f32[128,2048]{1,0:T(8,128)S(1)}, bf16[2,1601,1024]{2,1,0:T(8,128)(2,1)}) custom-call(s32[2]{0:T(128)S(1)} %pad_add_fusion.3.at_ref, bf16[1,128,2048]{2,1,0:T(8,128)(2,1)S(1)} %copy-done.9, bf16[1,128,2048]{2,1,0:T(8,128)(2,1)S(1)} %copy-done.3, bf16[2,1601,1024]{2,1,0:T(8,128)(2,1)} %bitcast.115, ...), custom_call_target="tpu_custom_call", output_to_operand_aliasing={{1}: (7, {})} | custom-call | flops 8393850880 | bytes 3278848 | tf_op jit(solution)/shard_map/backward_group/pallas_call | solution.py:209
  154.6 9.9 %collective-permute-start.17 = (bf16[128,2048]{1,0:T(8,128)(2,1)S(1)}, bf16[128,2048]{1,0:T(8,128)(2,1)S(1)}, u32[]{:S(2)}, u32[]{:S(2)}) collective-permute-start(bf16[128,2048]{1,0:T(8,128)(2,1)S(1)} %fusion.2), channel_id=1, source_target_pairs={{0,4},{4,8},{8,12},{12,16},{16,20},{20,24},{24,28},{1,5},{5,9},{9,... | collective-permute-start | bytes 1572872 | tf_op jit(solution)/shard_map/ppermute | solution.py:27
  165.0 11.2 %backward_group.7 = (f32[128,2048]{1,0:T(8,128)S(1)}, bf16[2,1601,1024]{2,1,0:T(8,128)(2,1)}) custom-call(s32[2]{0:T(128)S(1)} %get-tuple-element.150.at_ref, bf16[1,128,2048]{2,1,0:T(8,128)(2,1)S(1)} %fusion.6.q_ref, bf16[1,128,2048]{2,1,0:T(8,128)(2,1)S(1)} %select_bitcast_fusion.g_ref, ...), custom_call_target="tpu_custom_call", output_to_operand_aliasing={{1}: (7, {})} | custom-call | flops 8393850880 | bytes 3278848 | tf_op jit(solution)/shard_map/backward_group/pallas_call | solution.py:209
  176.2 4.5 %collective-permute-done.20 = bf16[128,2048]{1,0:T(8,128)(2,1)S(1)} collective-permute-done((bf16[128,2048]{1,0:T(8,128)(2,1)S(1)}, bf16[128,2048]{1,0:T(8,128)(2,1)S(1)}, u32[]{:S(2)}, u32[]{:S(2)}) %collective-permute-start.20) | collective-permute-done | bytes 524320 | tf_op jit(solution)/shard_map/ppermute | solution.py:22
  180.8 4.5 %collective-permute-start.21 = (bf16[128,2048]{1,0:T(8,128)(2,1)S(1)}, bf16[128,2048]{1,0:T(8,128)(2,1)S(1)}, u32[]{:S(2)}, u32[]{:S(2)}) collective-permute-start(bf16[128,2048]{1,0:T(8,128)(2,1)S(1)} %fusion.5), channel_id=1, source_target_pairs={{0,4},{4,8},{8,12},{12,16},{16,20},{20,24},{24,28},{1,5},{5,9},{9,... | collective-permute-start | bytes 1572872 | tf_op jit(solution)/shard_map/ppermute | solution.py:27
  185.3 2.9 %copy-done.1 = bf16[2,1601,1024]{2,1,0:T(8,128)(2,1)S(1)} copy-done((bf16[2,1601,1024]{2,1,0:T(8,128)(2,1)S(1)}, bf16[2,1601,1024]{2,1,0:T(8,128)(2,1)}, u32[]{:S(2)}) %copy-start.1) | copy-done | bytes 6557720
  188.2 5.8 %join_pairs.1 = bf16[1601,2,1024]{2,1,0:T(2,128)(2,1)} custom-call(bf16[2,1601,1024]{2,1,0:T(8,128)(2,1)S(1)} %copy-done.1), custom_call_target="tpu_custom_call" | custom-call | bytes 26230784 | tf_op jit(solution)/shard_map/join_pairs/pallas_call | solution.py:59
  (112 shorter events, 42.2 us)
Async XLA Ops:
  1.7 8.6 %collective-permute-start = (bf16[128,1024]{1,0:T(8,128)(2,1)S(1)}, bf16[128,1024]{1,0:T(8,128)(2,1)S(1)}, u32[]{:S(2)}, u32[]{:S(2)}) collective-permute-start(bf16[128,1024]{1,0:T(8,128)(2,1)S(1)} %get-tuple-element.114), channel_id=1, source_target_pairs={{4,0},{8,4},{12,8},{16,12},{20,16},{24,20},{28,24},{5,1},{9,5},{13... | collective-permute-start | bytes 786440 | tf_op jit(solution)/shard_map/ppermute | solution.py:27
  3.7 11.6 %collective-permute-start.1 = (bf16[128,1024]{1,0:T(8,128)(2,1)S(1)}, bf16[128,1024]{1,0:T(8,128)(2,1)S(1)}, u32[]{:S(2)}, u32[]{:S(2)}) collective-permute-start(bf16[128,1024]{1,0:T(8,128)(2,1)S(1)} %get-tuple-element.115), channel_id=1, source_target_pairs={{4,0},{8,4},{12,8},{16,12},{20,16},{24,20},{28,24},{5,1},{9,5},{13... | collective-permute-start | bytes 786440 | tf_op jit(solution)/shard_map/ppermute | solution.py:27
  11.4 10.8 %collective-permute-start.2 = (bf16[128,2048]{1,0:T(8,128)(2,1)S(1)}, bf16[128,2048]{1,0:T(8,128)(2,1)S(1)}, u32[]{:S(2)}, u32[]{:S(2)}) collective-permute-start(bf16[128,2048]{1,0:T(8,128)(2,1)S(1)} %multiply_convert_fusion), channel_id=1, source_target_pairs={{4,0},{8,4},{12,8},{16,12},{20,16},{24,20},{28,24},{5,1},{9,5},{13... | collective-permute-start | bytes 1572872 | tf_op jit(solution)/shard_map/ppermute | solution.py:27
  16.5 16.1 %collective-permute-start.3 = (bf16[1,128,2048]{2,1,0:T(8,128)(2,1)S(1)}, bf16[1,128,2048]{2,1,0:T(8,128)(2,1)S(1)}, u32[]{:S(2)}, u32[]{:S(2)}) collective-permute-start(bf16[1,128,2048]{2,1,0:T(8,128)(2,1)S(1)} %fusion.6.q_ref), channel_id=1, source_target_pairs={{0,1},{1,2},{2,3},{3,0},{4,5},{5,6},{6,7},{7,4},{8,9},{9,10},{10,1... | collective-permute-start | bytes 1572872 | tf_op jit(solution)/shard_map/ppermute | solution.py:22
  23.5 20.2 %collective-permute-start.4 = (bf16[1,128,2048]{2,1,0:T(8,128)(2,1)S(1)}, bf16[1,128,2048]{2,1,0:T(8,128)(2,1)S(1)}, u32[]{:S(2)}, u32[]{:S(2)}) collective-permute-start(bf16[1,128,2048]{2,1,0:T(8,128)(2,1)S(1)} %select_bitcast_fusion.g_ref), channel_id=1, source_target_pairs={{0,1},{1,2},{2,3},{3,0},{4,5},{5,6},{6,7},{7,4},{8,9},{9,10},{10,1... | collective-permute-start | bytes 1572872 | tf_op jit(solution)/shard_map/ppermute | solution.py:22
  32.7 22.2 %collective-permute-start.6 = (bf16[1,128,2048]{2,1,0:T(8,128)(2,1)S(1)}, bf16[1,128,2048]{2,1,0:T(8,128)(2,1)S(1)}, u32[]{:S(2)}, u32[]{:S(2)}) collective-permute-start(bf16[1,128,2048]{2,1,0:T(8,128)(2,1)S(1)} %collective-permute-done.3.q_ref), channel_id=1, source_target_pairs={{0,1},{1,2},{2,3},{3,0},{4,5},{5,6},{6,7},{7,4},{8,9},{9,10},{10,1... | collective-permute-start | bytes 1572872 | tf_op jit(solution)/shard_map/ppermute | solution.py:22
  43.7 30.1 %copy-start.4 = (bf16[1,128,2048]{2,1,0:T(8,128)(2,1)}, bf16[1,128,2048]{2,1,0:T(8,128)(2,1)S(1)}, u32[]{:S(2)}) copy-start(bf16[1,128,2048]{2,1,0:T(8,128)(2,1)S(1)} %collective-permute-done.4.g_ref) | copy-start | bytes 1572868
  43.7 22.5 %collective-permute-start.5 = (bf16[1,128,2048]{2,1,0:T(8,128)(2,1)S(1)}, bf16[1,128,2048]{2,1,0:T(8,128)(2,1)S(1)}, u32[]{:S(2)}, u32[]{:S(2)}) collective-permute-start(bf16[1,128,2048]{2,1,0:T(8,128)(2,1)S(1)} %collective-permute-done.4.g_ref), channel_id=1, source_target_pairs={{0,1},{1,2},{2,3},{3,0},{4,5},{5,6},{6,7},{7,4},{8,9},{9,10},{10,1... | collective-permute-start | bytes 1572872 | tf_op jit(solution)/shard_map/ppermute | solution.py:22
  54.9 22.5 %collective-permute-start.8 = (bf16[1,128,2048]{2,1,0:T(8,128)(2,1)S(1)}, bf16[1,128,2048]{2,1,0:T(8,128)(2,1)S(1)}, u32[]{:S(2)}, u32[]{:S(2)}) collective-permute-start(bf16[1,128,2048]{2,1,0:T(8,128)(2,1)S(1)} %collective-permute-done.6.q_ref), channel_id=1, source_target_pairs={{0,1},{1,2},{2,3},{3,0},{4,5},{5,6},{6,7},{7,4},{8,9},{9,10},{10,1... | collective-permute-start | bytes 1572872 | tf_op jit(solution)/shard_map/ppermute | solution.py:22
  66.2 19.3 %collective-permute-start.7 = (bf16[1,128,2048]{2,1,0:T(8,128)(2,1)S(1)}, bf16[1,128,2048]{2,1,0:T(8,128)(2,1)S(1)}, u32[]{:S(2)}, u32[]{:S(2)}) collective-permute-start(bf16[1,128,2048]{2,1,0:T(8,128)(2,1)S(1)} %collective-permute-done.5.g_ref), channel_id=1, source_target_pairs={{0,1},{1,2},{2,3},{3,0},{4,5},{5,6},{6,7},{7,4},{8,9},{9,10},{10,1... | collective-permute-start | bytes 1572872 | tf_op jit(solution)/shard_map/ppermute | solution.py:22
  87.7 3.8 %collective-permute-start.11 = (f32[2,4,2,8,128]{4,3,2,1,0:T(8,128)S(1)}, f32[2,4,2,8,128]{4,3,2,1,0:T(8,128)S(1)}, u32[]{:S(2)}, u32[]{:S(2)}) collective-permute-start(f32[2,4,2,8,128]{4,3,2,1,0:T(8,128)S(1)} %pad_maximum_fusion.1), channel_id=1, source_target_pairs={{0,3},{1,0},{2,1},{3,2},{4,7},{5,4},{6,5},{7,6},{8,11},{9,8},{10,9... | collective-permute-start | bytes 196616 | tf_op jit(solution)/shard_map/ppermute | solution.py:22
  89.5 6.0 %collective-permute-start.10 = (f32[2,4,2,8,128]{4,3,2,1,0:T(8,128)S(1)}, f32[2,4,2,8,128]{4,3,2,1,0:T(8,128)S(1)}, u32[]{:S(2)}, u32[]{:S(2)}) collective-permute-start(f32[2,4,2,8,128]{4,3,2,1,0:T(8,128)S(1)} %pad_maximum_fusion.1), channel_id=1, source_target_pairs={{0,2},{1,3},{2,0},{3,1},{4,6},{5,7},{6,4},{7,5},{8,10},{9,11},{10,... | collective-permute-start | bytes 196616 | tf_op jit(solution)/shard_map/ppermute | solution.py:22
  89.5 6.0 %collective-permute-start.9 = (f32[2,4,2,8,128]{4,3,2,1,0:T(8,128)S(1)}, f32[2,4,2,8,128]{4,3,2,1,0:T(8,128)S(1)}, u32[]{:S(2)}, u32[]{:S(2)}) collective-permute-start(f32[2,4,2,8,128]{4,3,2,1,0:T(8,128)S(1)} %pad_maximum_fusion.1), channel_id=1, source_target_pairs={{0,1},{1,2},{2,3},{3,0},{4,5},{5,6},{6,7},{7,4},{8,9},{9,10},{10,1... | collective-permute-start | bytes 196616 | tf_op jit(solution)/shard_map/ppermute | solution.py:22
  95.6 15.2 %collective-permute-start.14 = (bf16[128,2048]{1,0:T(8,128)(2,1)}, bf16[128,2048]{1,0:T(8,128)(2,1)S(1)}, u32[]{:S(2)}, u32[]{:S(2)}) collective-permute-start(bf16[128,2048]{1,0:T(8,128)(2,1)} %copy-done.12), channel_id=1, source_target_pairs={{0,1},{1,2},{2,3},{3,0},{4,5},{5,6},{6,7},{7,4},{8,9},{9,10},{10,1... | collective-permute-start | bytes 1572872 | tf_op jit(solution)/shard_map/ppermute | solution.py:22
  95.8 10.7 %collective-permute-start.13 = (f32[2,4,2,8,128]{4,3,2,1,0:T(8,128)S(1)}, f32[2,4,2,8,128]{4,3,2,1,0:T(8,128)S(1)}, u32[]{:S(2)}, u32[]{:S(2)}) collective-permute-start(f32[2,4,2,8,128]{4,3,2,1,0:T(8,128)S(1)} %pad_maximum_fusion.3), channel_id=1, source_target_pairs={{4,0},{8,4},{12,8},{16,12},{20,16},{24,20},{28,24},{5,1},{9,5},{13... | collective-permute-start | bytes 196616 | tf_op jit(solution)/shard_map/ppermute | solution.py:27
  98.1 9.4 %collective-permute-start.12 = (f32[2,4,2,8,128]{4,3,2,1,0:T(8,128)S(1)}, f32[2,4,2,8,128]{4,3,2,1,0:T(8,128)S(1)}, u32[]{:S(2)}, u32[]{:S(2)}) collective-permute-start(f32[2,4,2,8,128]{4,3,2,1,0:T(8,128)S(1)} %pad_maximum_fusion.2), channel_id=1, source_target_pairs={{0,4},{4,8},{8,12},{12,16},{16,20},{20,24},{24,28},{1,5},{5,9},{9,... | collective-permute-start | bytes 196616 | tf_op jit(solution)/shard_map/ppermute | solution.py:27
  112.2 14.0 %collective-permute-start.15 = (bf16[128,2048]{1,0:T(8,128)(2,1)S(1)}, bf16[128,2048]{1,0:T(8,128)(2,1)S(1)}, u32[]{:S(2)}, u32[]{:S(2)}) collective-permute-start(bf16[128,2048]{1,0:T(8,128)(2,1)S(1)} %mix_group.3), channel_id=1, source_target_pairs={{0,1},{1,2},{2,3},{3,0},{4,5},{5,6},{6,7},{7,4},{8,9},{9,10},{10,1... | collective-permute-start | bytes 1572872 | tf_op jit(solution)/shard_map/ppermute | solution.py:22
  125.5 14.0 %collective-permute-start.18 = (bf16[128,2048]{1,0:T(8,128)(2,1)S(1)}, bf16[128,2048]{1,0:T(8,128)(2,1)S(1)}, u32[]{:S(2)}, u32[]{:S(2)}) collective-permute-start(bf16[128,2048]{1,0:T(8,128)(2,1)S(1)} %convert_element_type.59), channel_id=1, source_target_pairs={{0,1},{1,2},{2,3},{3,0},{4,5},{5,6},{6,7},{7,4},{8,9},{9,10},{10,1... | collective-permute-start | bytes 1572872 | tf_op jit(solution)/shard_map/ppermute | solution.py:22
  127.4 25.8 %collective-permute-start.16 = (bf16[128,2048]{1,0:T(8,128)(2,1)S(1)}, bf16[128,2048]{1,0:T(8,128)(2,1)S(1)}, u32[]{:S(2)}, u32[]{:S(2)}) collective-permute-start(bf16[128,2048]{1,0:T(8,128)(2,1)S(1)} %mix_group.4), channel_id=1, source_target_pairs={{0,1},{1,2},{2,3},{3,0},{4,5},{5,6},{6,7},{7,4},{8,9},{9,10},{10,1... | collective-permute-start | bytes 1572872 | tf_op jit(solution)/shard_map/ppermute | solution.py:22
  127.8 14.3 %copy-start.9 = (bf16[1,128,2048]{2,1,0:T(8,128)(2,1)S(1)}, bf16[1,128,2048]{2,1,0:T(8,128)(2,1)}, u32[]{:S(2)}) copy-start(bf16[1,128,2048]{2,1,0:T(8,128)(2,1)} %copy-done.8) | copy-start | bytes 1572868
  139.7 24.9 %collective-permute-start.19 = (bf16[128,2048]{1,0:T(8,128)(2,1)S(1)}, bf16[128,2048]{1,0:T(8,128)(2,1)S(1)}, u32[]{:S(2)}, u32[]{:S(2)}) collective-permute-start(bf16[128,2048]{1,0:T(8,128)(2,1)S(1)} %add_convert_fusion.2), channel_id=1, source_target_pairs={{0,1},{1,2},{2,3},{3,0},{4,5},{5,6},{6,7},{7,4},{8,9},{9,10},{10,1... | collective-permute-start | bytes 1572872 | tf_op jit(solution)/shard_map/ppermute | solution.py:22
  154.6 21.6 %collective-permute-start.17 = (bf16[128,2048]{1,0:T(8,128)(2,1)S(1)}, bf16[128,2048]{1,0:T(8,128)(2,1)S(1)}, u32[]{:S(2)}, u32[]{:S(2)}) collective-permute-start(bf16[128,2048]{1,0:T(8,128)(2,1)S(1)} %fusion.2), channel_id=1, source_target_pairs={{0,4},{4,8},{8,12},{12,16},{16,20},{20,24},{24,28},{1,5},{5,9},{9,... | collective-permute-start | bytes 1572872 | tf_op jit(solution)/shard_map/ppermute | solution.py:27
  164.7 16.0 %collective-permute-start.20 = (bf16[128,2048]{1,0:T(8,128)(2,1)S(1)}, bf16[128,2048]{1,0:T(8,128)(2,1)S(1)}, u32[]{:S(2)}, u32[]{:S(2)}) collective-permute-start(bf16[128,2048]{1,0:T(8,128)(2,1)S(1)} %add_convert_fusion.1), channel_id=1, source_target_pairs={{0,1},{1,2},{2,3},{3,0},{4,5},{5,6},{6,7},{7,4},{8,9},{9,10},{10,1... | collective-permute-start | bytes 1572872 | tf_op jit(solution)/shard_map/ppermute | solution.py:22
  180.8 13.2 %collective-permute-start.21 = (bf16[128,2048]{1,0:T(8,128)(2,1)S(1)}, bf16[128,2048]{1,0:T(8,128)(2,1)S(1)}, u32[]{:S(2)}, u32[]{:S(2)}) collective-permute-start(bf16[128,2048]{1,0:T(8,128)(2,1)S(1)} %fusion.5), channel_id=1, source_target_pairs={{0,4},{4,8},{8,12},{12,16},{16,20},{20,24},{24,28},{1,5},{5,9},{9,... | collective-permute-start | bytes 1572872 | tf_op jit(solution)/shard_map/ppermute | solution.py:27
  (11 other events, 61.0 us)
